TPU v7x, 32 devices: a whole 2x2x4 slice. The times are simulated.
32 devices in a mesh: depth: 4 (over x, core), sx: 4 (over z), sy: 2 (over y).
Axes of the slice: x: 2, y: 2, z: 4, core: 2. Of those that a mesh axis runs over, the one named last changes fastest.
Arguments:
- density: float32 [128, 64, 1024], P('sx', 'sy', 'depth'), may hold values from -6 to 6
- kernel_taps: bfloat16 [2, 33], replicated, may hold values from 0.099609375 to 0.3984375
- tf_centre: float32 [8, 4], replicated, may hold values from -2 to 2
- tf_width: float32 [8, 4], replicated, may hold values from 0.4 to 1.5
- tf_color: float32 [8, 4, 3], replicated, may hold values from 0.05 to 1
- tf_opacity: float32 [8, 4], replicated, may hold values from 0.0005 to 0.004
- brick_tf: int32 [8, 4, 8], P('sx', 'sy', 'depth'), may hold values from 0 to 7
- view_order: int32 [8, 4], P('sx', 'sy'), may hold values from 0 to 1
Outputs:
- picture: float32 [4, 4, 4, 8, 64], P(None, 'sx', 'depth', None, 'sy')
Inputs may be any that keep to these rules, and one draw needn't show every extreme that they name: `view_order`: 0: the viewer of that column of bricks faces z = 0; 1: it faces z = 1023.
All inputs are finite; a program needn't handle non-finite values.
Results may differ from a plain program's by a relative error of at most 0.0003.
Values may be sent and summed in bfloat16 or wider, within the bound.
No kernel may reach another device: no remote copies, remote signals or barrier semaphores. Data moves between devices by JAX's collectives and lax.ppermute only.
A program may use at most 64 MiB of HBM per device.

v0:
```python
import functools
import math
import jax
import jax.numpy as jnp
from jax import lax
from jax.experimental import pallas as pl
from jax.experimental.pallas import tpu as pltpu
from jax.sharding import PartitionSpec as P

LOG2E = math.log2(math.e)
VMEM = pl.BlockSpec(memory_space=pltpu.VMEM)
SMEM = pl.BlockSpec(memory_space=pltpu.SMEM)
ANY = pl.BlockSpec(memory_space=pl.ANY)
VMEM_LIMIT = 40 * 1024 * 1024


def swap_rounds(count):
    rounds = []
    for first in (0, 1):
        pairs = [(i, i + 1) for i in range(first, count - 1, 2)]
        if pairs:
            rounds.append([(a, b) for a, b in pairs] + [(b, a) for a, b in pairs])
    return rounds


def strips_kernel(rim, y_rounds, x_parity, y_parity, density, xs1, xs2, *ys):
    px, py = x_parity(), y_parity()
    first = pl.ds(rim * (1 - px), rim)
    second = pl.ds(rim * px, rim)
    for r in range(y_rounds):
        group = pl.ds(pl.multiple_of(rim * (1 - py if r == 0 else py), rim), rim)
        ys[2 * r][...] = density[first, group, :].astype(jnp.bfloat16)
        ys[2 * r + 1][...] = density[second, group, :].astype(jnp.bfloat16)
    xs1[...] = density[first].astype(jnp.bfloat16)
    xs2[...] = density[second].astype(jnp.bfloat16)


def iota(shape, dim):
    return lax.broadcasted_iota(jnp.int32, shape, dim)


def toeplitz(taps, rim):
    return pltpu.roll(jnp.broadcast_to(taps, (rim, 128)), 0, 1, stride=1, stride_axis=0)


def blur_matrices(rim, taps):
    size = rim * rim
    f32, bf16 = jnp.float32, jnp.bfloat16
    row_hi = iota((size, rim), 0) // rim == iota((size, rim), 1)
    row_lo = iota((size, rim), 0) % rim == iota((size, rim), 1)
    col = iota((128, 3 * size), 1)
    src = iota((128, 3 * size), 0)
    col_x = col // rim == src
    col_y = (col // size) * rim + col % rim == src
    tx = toeplitz(taps[0:1], rim).astype(bf16)
    ty = toeplitz(taps[1:2] * 0.5, rim).astype(bf16)
    wide_x = jnp.dot(tx, col_x.astype(f32).astype(bf16), preferred_element_type=f32).astype(bf16)
    wide_y = jnp.dot(ty, col_y.astype(f32).astype(bf16), preferred_element_type=f32).astype(bf16)
    full_x = jnp.dot(row_hi.astype(f32).astype(bf16), wide_x, preferred_element_type=f32)
    full_y = jnp.dot(row_lo.astype(f32).astype(bf16), wide_y, preferred_element_type=f32)
    r, c = iota((size, 3 * size), 0), iota((size, 3 * size), 1)
    dd = jnp.where(r % rim == c % rim, full_x, 0.0)
    ee = jnp.where(r // rim == (c // rim) % rim, full_y, 0.0)
    return dd.astype(bf16), ee.astype(bf16)


def cells_kernel(
    rim, bumps, taps, centre, width, colour, opacity, brick_tf, view_order, density,
    coarse, g0, g1, g2, total, dd, ee, optical_s, e0, e1, e2
):
    by, bx = pl.program_id(0), pl.program_id(1)
    bricks = brick_tf.shape[2]
    rows_x, rows_y, rows_z = density.shape
    depth = rows_z // bricks
    f32, bf16 = jnp.float32, jnp.bfloat16

    @pl.when(jnp.logical_and(by == 0, bx == 0))
    def _():
        dd_v, ee_v = blur_matrices(rim, taps[...])
        dd[...] = dd_v
        ee[...] = ee_v

    emitted = (e0, e1, e2)
    coarse[...] = density[...].astype(bf16)
    for bz in range(bricks):
        zs = slice(bz * depth, (bz + 1) * depth)
        k = brick_tf[bx, by, bz]
        cen, neg, opa, col = [], [], [], []
        for j in range(bumps):
            cen.append(centre[k, j])
            wide = jnp.full((8, depth), width[k, j], f32)
            neg.append((-LOG2E / (wide * wide))[None])
            opa.append(opacity[k, j] * (-LOG2E))
            col.append([colour[k, 3 * j + c] * 0.5 for c in range(3)])
        for x in range(rows_x):
            d = density[x, :, zs].reshape(rows_y // 8, 8, depth)
            opt, em = None, [None] * 3
            for j in range(bumps):
                w = d - cen[j]
                b = jnp.exp2((w * w) * neg[j])
                opt = opa[j] * b if opt is None else opt + opa[j] * b
                for c in range(3):
                    em[c] = col[j][c] * b if em[c] is None else em[c] + col[j][c] * b
            rows = slice(x * rows_y, (x + 1) * rows_y)
            optical_s[rows, zs] = opt.reshape(rows_y, depth)
            for c in range(3):
                emitted[c][rows, zs] = em[c].reshape(rows_y, depth)
    order = view_order[bx, by]
    zr, zc = iota((rows_z, rows_z), 0), iota((rows_z, rows_z), 1)
    sign = 1 - 2 * order
    tri = jnp.where((zc - zr) * sign > 0, 1.0, 0.0).astype(bf16)
    opt = optical_s[...]
    hi = opt.astype(bf16)
    lo = (opt - hi.astype(f32)).astype(bf16)
    ahead = jnp.dot(hi, tri, preferred_element_type=f32) + jnp.dot(lo, tri, preferred_element_type=f32)
    weight = jnp.exp2(ahead) * (1.0 - jnp.exp2(opt))
    for c, out in enumerate((g0, g1, g2)):
        out[...] = (weight * emitted[c][...]).reshape(rows_x, rows_y, rows_z)
    folded = opt[:, :depth]
    for bz in range(1, bricks):
        folded = folded + opt[:, bz * depth:(bz + 1) * depth]
    summed = jnp.sum(folded.reshape(rows_x, rows_y, depth), axis=2, keepdims=True)
    lane = iota((rows_y, 128), 1)
    acc = jnp.zeros((rows_y, 128), f32)
    for x in range(rows_x):
        acc = jnp.where(lane == bx * rows_x + x, summed[x], acc)

    @pl.when(bx == 0)
    def _():
        total[...] = acc

    @pl.when(bx > 0)
    def _():
        total[...] += acc


def image_kernel(
    rim, depth_count, x_rounds, y_rounds, x_parity, y_parity, depth_index, *refs
):
    refs = list(refs)
    coarse, g0, g1, g2, total, dd, ee = refs[:7]
    refs = refs[7:]
    xr = refs[:x_rounds]
    refs = refs[x_rounds:]
    strips = refs[:2 * y_rounds]
    refs = refs[2 * y_rounds:]
    corners = refs[:x_rounds * y_rounds]
    refs = refs[x_rounds * y_rounds:]
    outs = refs[:depth_count]
    cx, ac, img, sems = refs[depth_count:]
    f32, bf16 = jnp.float32, jnp.bfloat16
    px, py, me = x_parity(), y_parity(), depth_index()
    rows_x, rows_y, rows_z = coarse.shape
    half = rows_x // rim
    groups = rows_y // rim

    def y_cols(r):
        return slice(rows_y + r * rim, rows_y + (r + 1) * rim)

    copies = [(coarse, cx.at[rim:rim + rows_x, 0:rows_y])]
    for n in range(x_rounds):
        at = (rows_x + rim) * ((1 - px) if n == 0 else px)
        copies.append((xr[n], cx.at[pl.ds(at, rim), 0:rows_y]))
    for r in range(y_rounds):
        for n in range(2):
            at = rim + rim * ((1 - px) if n == 0 else px)
            copies.append((strips[2 * r + n], cx.at[pl.ds(at, rim), y_cols(r)]))
        for n in range(x_rounds):
            at = (rows_x + rim) * ((1 - px) if n == 0 else px)
            copies.append((corners[r * x_rounds + n], cx.at[pl.ds(at, rim), y_cols(r)]))
    started = []
    for i, (src, dst) in enumerate(copies):
        copy = pltpu.make_async_copy(src, dst, sems.at[i])
        copy.start()
        started.append(copy)
    if x_rounds < 2:
        for n in range(x_rounds, 2):
            at = (rows_x + rim) * ((1 - px) if n == 0 else px)
            cx[pl.ds(at, rim)] = jnp.zeros((rim,) + cx.shape[1:], bf16)
    for r in range(y_rounds, 2):
        slot = (groups + 1) * ((1 - py) if r == 0 else py)
        ac[pl.ds(slot, 1)] = jnp.zeros((1,) + ac.shape[1:], bf16)
    for copy in started:
        copy.wait()
    for g in range(groups + y_rounds):
        if g < groups:
            slot = g + 1
        else:
            slot = (groups + 1) * ((1 - py) if g == groups else py)
        for h in range(half):
            rhs = cx[h * rim:(h + 3) * rim, g * rim:(g + 1) * rim, :].reshape(3 * rim * rim, rows_z)
            across = jnp.dot(dd[...], rhs, preferred_element_type=f32).astype(bf16)
            ac[slot, h * rim:(h + 1) * rim] = across.reshape(rim, rim, rows_z)
    lane = iota((rim, 128), 1)
    for g in range(groups):
        accs = [jnp.zeros((rim, 128), f32) for c in range(3)]
        for h in range(half):
            rhs = ac[g:g + 3, h * rim:(h + 1) * rim].reshape(3 * rim * rim, rows_z)
            occ = jnp.dot(ee[...], rhs, preferred_element_type=f32)
            shade = (1.0 - jnp.tanh(occ)).reshape(rim, rim, rows_z)
            for c, gref in enumerate((g0, g1, g2)):
                v = shade * gref[h * rim:(h + 1) * rim, g * rim:(g + 1) * rim, :]
                folded = v[:, :, :128]
                for z in range(128, rows_z, 128):
                    folded = folded + v[:, :, z:z + 128]
                summed = jnp.sum(folded, axis=2, keepdims=True)
                for x in range(rim):
                    accs[c] = jnp.where(lane == h * rim + x, summed[x], accs[c])
        for c in range(3):
            img[c, g * rim:(g + 1) * rim, :] = accs[c]
    img[3] = jnp.exp2(total[...])
    for c in range(4):
        img[4 + c, 0:rows_x, 0:rows_y] = img[c].T[:rows_x, :]
    block = rows_x // depth_count
    for k in range(depth_count):
        at = pl.multiple_of((me ^ k) * block, block)
        outs[k][...] = img[4:8, pl.ds(at, block), 0:rows_y]


def picture_kernel(rim, depth_count, block, depth_index, view_order, *refs):
    parts = [ref[...] for ref in refs[:depth_count]]
    out = refs[depth_count]
    me = depth_index()
    shape = parts[0].shape[1:]
    brick = (me * block) // rim
    order = jnp.zeros(shape, jnp.int32)
    for y in range(view_order.shape[1]):
        order = jnp.where(iota(shape, 1) // rim == y, view_order[brick, y], order)
    bit = 0
    while len(parts) > 1:
        mine = (me >> bit & 1) == order
        merged = []
        for a, b in zip(parts[::2], parts[1::2]):
            front = jnp.where(mine[None], a, b)
            back = jnp.where(mine[None], b, a)
            merged.append(
                jnp.concatenate([front[:3] + front[3:] * back[:3], front[3:] * back[3:]])
            )
        parts = merged
        bit += 1
    final = jnp.concatenate([parts[0][:3], 1.0 - parts[0][3:]])
    out[...] = final.reshape(out.shape)


def per_device(
    density, kernel_taps, tf_centre, tf_width, tf_color, tf_opacity, brick_tf, view_order
):
    f32, bf16 = jnp.float32, jnp.bfloat16
    rows_x, rows_y, rows_z = density.shape
    rim = (kernel_taps.shape[1] - 1) // 2
    bumps = tf_centre.shape[1]
    bricks = brick_tf.shape
    depth_count = lax.axis_size("depth")
    x_swaps = swap_rounds(lax.axis_size("sx"))
    y_swaps = swap_rounds(lax.axis_size("sy"))
    x_parity = lambda: lax.rem(lax.axis_index("sx"), 2)
    y_parity = lambda: lax.rem(lax.axis_index("sy"), 2)
    depth_index = lambda: lax.axis_index("depth")
    params = pltpu.CompilerParams(vmem_limit_bytes=VMEM_LIMIT)
    struct = jax.ShapeDtypeStruct

    sends = pl.pallas_call(
        functools.partial(strips_kernel, rim, len(y_swaps), x_parity, y_parity),
        out_shape=[struct((rim, rows_y, rows_z), bf16)] * 2
        + [struct((rim, rim, rows_z), bf16)] * (2 * len(y_swaps)),
        in_specs=[VMEM],
        out_specs=[VMEM] * (2 + 2 * len(y_swaps)),
        compiler_params=params,
        name="strips",
    )(density)
    strips = [
        lax.ppermute(piece, "sy", y_swaps[i // 2]) for i, piece in enumerate(sends[2:])
    ]
    x_halos = [lax.ppermute(piece, "sx", swaps) for piece, swaps in zip(sends[:2], x_swaps)]
    corners = [
        lax.ppermute(strips[2 * r + n], "sx", swaps)
        for r in range(len(y_swaps))
        for n, swaps in enumerate(x_swaps)
    ]

    size = rim * rim
    taps = jnp.pad(kernel_taps.astype(f32), ((0, 0), (0, 128 - kernel_taps.shape[1])))
    cell_block = pl.BlockSpec((rows_x // bricks[0], rows_y // bricks[1], rows_z), lambda y, x: (x, y, 0))
    whole = lambda shape: pl.BlockSpec(shape, lambda y, x: (0,) * len(shape))
    group_rows = (rows_x // bricks[0]) * (rows_y // bricks[1])
    coarse, g0, g1, g2, total, dd, ee = pl.pallas_call(
        functools.partial(cells_kernel, rim, bumps),
        grid=(bricks[1], bricks[0]),
        out_shape=[struct(density.shape, bf16)]
        + [struct(density.shape, f32)] * 3
        + [struct((rows_y, 128), f32)]
        + [struct((size, 3 * size), bf16)] * 2,
        in_specs=[whole((2, 128))] + [SMEM] * 6 + [cell_block],
        out_specs=[cell_block] * 4
        + [pl.BlockSpec((rows_y // bricks[1], 128), lambda y, x: (y, 0))]
        + [whole((size, 3 * size))] * 2,
        scratch_shapes=[pltpu.VMEM((group_rows, rows_z), f32)] * 4,
        compiler_params=params,
        cost_estimate=pl.CostEstimate(flops=density.size * 60, bytes_accessed=density.size * 20, transcendentals=density.size * 6),
        name="cells",
    )(taps, tf_centre, tf_width, tf_color.reshape(tf_color.shape[0], -1), tf_opacity, brick_tf, view_order, density)

    block = rows_x // depth_count
    n_copies = 1 + len(x_swaps) + 2 * len(y_swaps) + len(corners)
    parts = pl.pallas_call(
        functools.partial(
            image_kernel, rim, depth_count, len(x_swaps), len(y_swaps), x_parity, y_parity, depth_index
        ),
        out_shape=[struct((4, block, rows_y), f32)] * depth_count,
        in_specs=[ANY] + [VMEM] * 6 + [ANY] * (n_copies - 1),
        out_specs=[VMEM] * depth_count,
        scratch_shapes=[
            pltpu.VMEM((rows_x + 2 * rim, rows_y + rim * len(y_swaps), rows_z), bf16),
            pltpu.VMEM((rows_y // rim + 2, rows_x, rim, rows_z), bf16),
            pltpu.VMEM((8, rows_y, 128), f32),
            pltpu.SemaphoreType.DMA((n_copies,)),
        ],
        compiler_params=params,
        name="image",
    )(coarse, g0, g1, g2, total, dd, ee, *x_halos, *strips, *corners)
    pieces = [parts[0]] + [
        lax.ppermute(parts[k], "depth", [(i, i ^ k) for i in range(depth_count)])
        for k in range(1, depth_count)
    ]
    return pl.pallas_call(
        functools.partial(picture_kernel, rim, depth_count, block, depth_index),
        out_shape=struct((4, 1, 1, block, rows_y), f32),
        in_specs=[SMEM] + [VMEM] * depth_count,
        out_specs=VMEM,
        name="picture",
    )(view_order, *pieces)


def solution(mesh):
    return jax.shard_map(
        per_device,
        mesh=mesh,
        in_specs=(
            P("sx", "sy", "depth"),
            P(),
            P(),
            P(),
            P(),
            P(),
            P("sx", "sy", "depth"),
            P("sx", "sy"),
        ),
        out_specs=P(None, "sx", "depth", None, "sy"),
        check_vma=False,
    )
```

profile of v0, /device:TPU:13, one launch (start us, length us, event | category | flops | bytes accessed | tf_op | source)
XLA Modules:
  0.0 29.1 jit_solution(5548773465474297350)
XLA Ops:
  0.0 1.2 %copy-done = f32[32,32,256]{2,1,0:T(8,128)S(1)} copy-done((f32[32,32,256]{2,1,0:T(8,128)S(1)}, f32[32,32,256]{2,1,0:T(8,128)}, u32[]{:S(2)}) %copy-start) | copy-done | bytes 1048600
  1.3 0.3 %collective-permute-start.2 = (bf16[16,16,256]{2,1,0:T(8,128)(2,1)S(1)}, bf16[16,16,256]{2,1,0:T(8,128)(2,1)S(1)}, u32[]{:S(2)}, u32[]{:S(2)}) collective-permute-start(bf16[16,16,256]{2,1,0:T(8,128)(2,1)S(1)} %get-tuple-element.29), channel_id=1, source_target_pairs={{0,1},{1,0},{2,3},{3,2},{4,5},{5,4},{6,7},{7,6},{8,9},{9,8},{10,11... | collective-permute-start | bytes 393224 | tf_op jit(solution)/shard_map/ppermute | solution.py:272
  1.6 1.2 %collective-permute-start.3 = (bf16[16,16,256]{2,1,0:T(8,128)(2,1)S(1)}, bf16[16,16,256]{2,1,0:T(8,128)(2,1)S(1)}, u32[]{:S(2)}, u32[]{:S(2)}) collective-permute-start(bf16[16,16,256]{2,1,0:T(8,128)(2,1)S(1)} %get-tuple-element.30), channel_id=1, source_target_pairs={{0,1},{1,0},{2,3},{3,2},{4,5},{5,4},{6,7},{7,6},{8,9},{9,8},{10,11... | collective-permute-start | bytes 393224 | tf_op jit(solution)/shard_map/ppermute | solution.py:272
  2.8 0.2 collective-permute-start
  3.0 4.5 %collective-permute-start.1 = (bf16[16,32,256]{2,1,0:T(8,128)(2,1)S(1)}, bf16[16,32,256]{2,1,0:T(8,128)(2,1)S(1)}, u32[]{:S(2)}, u32[]{:S(2)}) collective-permute-start(bf16[16,32,256]{2,1,0:T(8,128)(2,1)S(1)} %get-tuple-element.28), channel_id=1, source_target_pairs={{2,4},{4,2},{3,5},{5,3},{10,12},{12,10},{11,13},{13,11},{18,20},{2... | collective-permute-start | bytes 786440 | tf_op jit(solution)/shard_map/ppermute | solution.py:274
  7.6 1.0 %collective-permute-done.3.refs_10_ = bf16[16,16,256]{2,1,0:T(8,128)(2,1)S(1)} collective-permute-done((bf16[16,16,256]{2,1,0:T(8,128)(2,1)S(1)}, bf16[16,16,256]{2,1,0:T(8,128)(2,1)S(1)}, u32[]{:S(2)}, u32[]{:S(2)}) %collective-permute-start.3) | collective-permute-done | bytes 131104 | tf_op jit(solution)/shard_map/ppermute | solution.py:272
  8.5 3.2 %collective-permute-start.5 = (bf16[16,16,256]{2,1,0:T(8,128)(2,1)S(1)}, bf16[16,16,256]{2,1,0:T(8,128)(2,1)S(1)}, u32[]{:S(2)}, u32[]{:S(2)}) collective-permute-start(bf16[16,16,256]{2,1,0:T(8,128)(2,1)S(1)} %collective-permute-done.3.refs_10_), channel_id=1, source_target_pairs={{2,4},{4,2},{3,5},{5,3},{10,12},{12,10},{11,13},{13,11},{18,20},{2... | collective-permute-start | bytes 393224 | tf_op jit(solution)/shard_map/ppermute | solution.py:276
  11.8 0.1 copy.15.centre
  11.8 0.1 copy.16.width
  11.9 0.1 copy.18.opacity
  12.0 0.5 %copy-done.8 = f32[8,4,3]{0,1,2:T(4,128)S(1)} copy-done((f32[8,4,3]{0,1,2:T(4,128)S(1)}, f32[8,4,3]{0,1,2:T(4,128)}, u32[]{:S(2)}) %copy-start.8) | copy-done | bytes 408
  12.5 0.1 copy.19
  12.7 0.6 %copy-done.12 = bf16[2,33]{1,0:T(2,128)(2,1)S(1)} copy-done((bf16[2,33]{1,0:T(2,128)(2,1)S(1)}, bf16[2,33]{1,0:T(2,128)(2,1)}, u32[]{:S(2)}) %copy-start.12) | copy-done | bytes 156
  13.3 0.6 %copy-done.3 = s32[2,2]{1,0:T(2,128)S(1)} copy-done((s32[2,2]{1,0:T(2,128)S(1)}, s32[2,2]{1,0:T(2,128)}, u32[]{:S(2)}) %copy-start.3) | copy-done | bytes 40
  14.0 4.3 %cells.1 = (bf16[32,32,256]{2,1,0:T(8,128)(2,1)S(1)}, f32[32,32,256]{2,1,0:T(8,128)S(1)}, f32[32,32,256]{2,1,0:T(8,128)S(1)}, f32[32,32,256]{2,1,0:T(8,128)S(1)}...) custom-call(f32[2,128]{1,0:T(2,128)S(1)} %pad_convert_fusion.taps, ...), custom_call_target="tpu_custom_call" | custom-call | flops 15728640 | bytes 5242880 | tf_op jit(solution)/shard_map/cells/pallas_call | solution.py:286
  18.3 2.0 %image.1 = (f32[4,8,32]{2,1,0:T(8,128)S(1)}, f32[4,8,32]{2,1,0:T(8,128)S(1)}, f32[4,8,32]{2,1,0:T(8,128)S(1)}, f32[4,8,32]{2,1,0:T(8,128)S(1)}) custom-call(bf16[32,32,256]{2,1,0:T(8,128)(2,1)S(1)} %get-tuple-element.20.refs_0_, f32[32,32,256]{2,1,0:T(8,128)S(1)} %get-tuple-element.21.refs_1_, f32[32,32,256]{2,1,0:T(8,128)S(1)} %get-tuple-element.22.refs_2_, ...), custom_call_target="tpu_custom_call" | custom-call | tf_op jit(solution)/shard_map/image/pallas_call | solution.py:305
  20.3 0.6 %copy-done.2 = f32[4,8,32]{2,1,0:T(8,128)} copy-done((f32[4,8,32]{2,1,0:T(8,128)}, f32[4,8,32]{2,1,0:T(8,128)S(1)}, u32[]{:S(2)}) %copy-start.2) | copy-done | bytes 4120
  20.9 1.8 %collective-permute-start.6 = (f32[4,8,32]{2,1,0:T(8,128)S(1)}, f32[4,8,32]{2,1,0:T(8,128)S(1)}, u32[]{:S(2)}, u32[]{:S(2)}) collective-permute-start(f32[4,8,32]{2,1,0:T(8,128)S(1)} %get-tuple-element.32), channel_id=1, source_target_pairs={{0,8},{8,0},{16,24},{24,16},{1,9},{9,1},{17,25},{25,17},{2,10},{10... | collective-permute-start | bytes 12296 | tf_op jit(solution)/shard_map/ppermute | solution.py:322
  22.7 1.2 %collective-permute-start.7 = (f32[4,8,32]{2,1,0:T(8,128)S(1)}, f32[4,8,32]{2,1,0:T(8,128)S(1)}, u32[]{:S(2)}, u32[]{:S(2)}) collective-permute-start(f32[4,8,32]{2,1,0:T(8,128)S(1)} %get-tuple-element.33), channel_id=1, source_target_pairs={{0,16},{8,24},{16,0},{24,8},{1,17},{9,25},{17,1},{25,9},{2,18},{10... | collective-permute-start | bytes 12296 | tf_op jit(solution)/shard_map/ppermute | solution.py:322
  23.9 0.4 %collective-permute-start.8 = (f32[4,8,32]{2,1,0:T(8,128)S(1)}, f32[4,8,32]{2,1,0:T(8,128)S(1)}, u32[]{:S(2)}, u32[]{:S(2)}) collective-permute-start(f32[4,8,32]{2,1,0:T(8,128)S(1)} %get-tuple-element.34), channel_id=1, source_target_pairs={{0,24},{8,16},{16,8},{24,0},{1,25},{9,17},{17,9},{25,1},{2,26},{10... | collective-permute-start | bytes 12296 | tf_op jit(solution)/shard_map/ppermute | solution.py:322
  24.3 0.9 %collective-permute-done.7.refs_2_ = f32[4,8,32]{2,1,0:T(8,128)S(1)} collective-permute-done((f32[4,8,32]{2,1,0:T(8,128)S(1)}, f32[4,8,32]{2,1,0:T(8,128)S(1)}, u32[]{:S(2)}, u32[]{:S(2)}) %collective-permute-start.7) | collective-permute-done | bytes 4128 | tf_op jit(solution)/shard_map/ppermute | solution.py:322
  25.3 1.8 %collective-permute-done.8.refs_3_ = f32[4,8,32]{2,1,0:T(8,128)S(1)} collective-permute-done((f32[4,8,32]{2,1,0:T(8,128)S(1)}, f32[4,8,32]{2,1,0:T(8,128)S(1)}, u32[]{:S(2)}, u32[]{:S(2)}) %collective-permute-start.8) | collective-permute-done | bytes 4128 | tf_op jit(solution)/shard_map/ppermute | solution.py:322
  27.1 0.6 %copy-done.7 = f32[4,8,32]{2,1,0:T(8,128)} copy-done((f32[4,8,32]{2,1,0:T(8,128)}, f32[4,8,32]{2,1,0:T(8,128)S(1)}, u32[]{:S(2)}) %copy-start.7) | copy-done | bytes 4120
  27.7 1.5 %picture.1 = f32[4,1,1,8,32]{4,3,2,1,0:T(8,128)} custom-call(s32[2,2]{1,0:T(2,128)} %view_order.3, f32[4,8,32]{2,1,0:T(8,128)} %copy-done.2, f32[4,8,32]{2,1,0:T(8,128)} %copy-done.5, f32[4,8,32]{2,1,0:T(8,128)} %copy-done.6, f32[4,8,32]{2,1,0:T(8,128)} %copy-done.7), custom_call_target="tpu_custom_call" | custom-call | tf_op jit(solution)/shard_map/picture/pallas_call | solution.py:325
  (30 shorter events, 0.3 us)
Async XLA Ops:
  0.0 1.2 %copy-start = (f32[32,32,256]{2,1,0:T(8,128)S(1)}, f32[32,32,256]{2,1,0:T(8,128)}, u32[]{:S(2)}) copy-start(f32[32,32,256]{2,1,0:T(8,128)} %density.3) | copy-start | bytes 3145732
  1.2 12.1 %copy-start.1 = (f32[32,32,256]{2,1,0:T(8,128)S(1)}, f32[32,32,256]{2,1,0:T(8,128)}, u32[]{:S(2)}) copy-start(f32[32,32,256]{2,1,0:T(8,128)} %density.3) | copy-start | bytes 3145732
  1.3 6.2 %collective-permute-start.2 = (bf16[16,16,256]{2,1,0:T(8,128)(2,1)S(1)}, bf16[16,16,256]{2,1,0:T(8,128)(2,1)S(1)}, u32[]{:S(2)}, u32[]{:S(2)}) collective-permute-start(bf16[16,16,256]{2,1,0:T(8,128)(2,1)S(1)} %get-tuple-element.29), channel_id=1, source_target_pairs={{0,1},{1,0},{2,3},{3,2},{4,5},{5,4},{6,7},{7,6},{8,9},{9,8},{10,11... | collective-permute-start | bytes 393224 | tf_op jit(solution)/shard_map/ppermute | solution.py:272
  1.6 10.3 %copy-start.11 = (f32[8,4]{0,1:T(4,128)S(1)}, f32[8,4]{0,1:T(4,128)}, u32[]{:S(2)}) copy-start(f32[8,4]{0,1:T(4,128)} %param.13) | copy-start | bytes 388
  1.6 10.1 %copy-start.9 = (f32[8,4]{0,1:T(4,128)S(1)}, f32[8,4]{0,1:T(4,128)}, u32[]{:S(2)}) copy-start(f32[8,4]{0,1:T(4,128)} %param.10) | copy-start | bytes 388
  1.6 6.9 %collective-permute-start.3 = (bf16[16,16,256]{2,1,0:T(8,128)(2,1)S(1)}, bf16[16,16,256]{2,1,0:T(8,128)(2,1)S(1)}, u32[]{:S(2)}, u32[]{:S(2)}) collective-permute-start(bf16[16,16,256]{2,1,0:T(8,128)(2,1)S(1)} %get-tuple-element.30), channel_id=1, source_target_pairs={{0,1},{1,0},{2,3},{3,2},{4,5},{5,4},{6,7},{7,6},{8,9},{9,8},{10,11... | collective-permute-start | bytes 393224 | tf_op jit(solution)/shard_map/ppermute | solution.py:272
  2.8 15.4 %collective-permute-start = (bf16[16,32,256]{2,1,0:T(8,128)(2,1)S(1)}, bf16[16,32,256]{2,1,0:T(8,128)(2,1)S(1)}, u32[]{:S(2)}, u32[]{:S(2)}) collective-permute-start(bf16[16,32,256]{2,1,0:T(8,128)(2,1)S(1)} %get-tuple-element.27), channel_id=1, source_target_pairs={{0,2},{4,6},{2,0},{6,4},{1,3},{5,7},{3,1},{7,5},{8,10},{12,14},{10... | collective-permute-start | bytes 786440 | tf_op jit(solution)/shard_map/ppermute | solution.py:274
  3.0 8.8 %copy-start.10 = (f32[8,4]{0,1:T(4,128)S(1)}, f32[8,4]{0,1:T(4,128)}, u32[]{:S(2)}) copy-start(f32[8,4]{0,1:T(4,128)} %param.11) | copy-start | bytes 388
  3.0 15.3 %collective-permute-start.1 = (bf16[16,32,256]{2,1,0:T(8,128)(2,1)S(1)}, bf16[16,32,256]{2,1,0:T(8,128)(2,1)S(1)}, u32[]{:S(2)}, u32[]{:S(2)}) collective-permute-start(bf16[16,32,256]{2,1,0:T(8,128)(2,1)S(1)} %get-tuple-element.28), channel_id=1, source_target_pairs={{2,4},{4,2},{3,5},{5,3},{10,12},{12,10},{11,13},{13,11},{18,20},{2... | collective-permute-start | bytes 786440 | tf_op jit(solution)/shard_map/ppermute | solution.py:274
  7.5 10.8 %collective-permute-start.4 = (bf16[16,16,256]{2,1,0:T(8,128)(2,1)S(1)}, bf16[16,16,256]{2,1,0:T(8,128)(2,1)S(1)}, u32[]{:S(2)}, u32[]{:S(2)}) collective-permute-start(bf16[16,16,256]{2,1,0:T(8,128)(2,1)S(1)} %collective-permute-done.2.refs_9_), channel_id=1, source_target_pairs={{0,2},{4,6},{2,0},{6,4},{1,3},{5,7},{3,1},{7,5},{8,10},{12,14},{10... | collective-permute-start | bytes 393224 | tf_op jit(solution)/shard_map/ppermute | solution.py:276
  8.5 9.7 %collective-permute-start.5 = (bf16[16,16,256]{2,1,0:T(8,128)(2,1)S(1)}, bf16[16,16,256]{2,1,0:T(8,128)(2,1)S(1)}, u32[]{:S(2)}, u32[]{:S(2)}) collective-permute-start(bf16[16,16,256]{2,1,0:T(8,128)(2,1)S(1)} %collective-permute-done.3.refs_10_), channel_id=1, source_target_pairs={{2,4},{4,2},{3,5},{5,3},{10,12},{12,10},{11,13},{13,11},{18,20},{2... | collective-permute-start | bytes 393224 | tf_op jit(solution)/shard_map/ppermute | solution.py:276
  11.8 0.7 %copy-start.8 = (f32[8,4,3]{0,1,2:T(4,128)S(1)}, f32[8,4,3]{0,1,2:T(4,128)}, u32[]{:S(2)}) copy-start(f32[8,4,3]{0,1,2:T(4,128)} %param.12) | copy-start | bytes 1156
  12.6 0.7 %copy-start.12 = (bf16[2,33]{1,0:T(2,128)(2,1)S(1)}, bf16[2,33]{1,0:T(2,128)(2,1)}, u32[]{:S(2)}) copy-start(bf16[2,33]{1,0:T(2,128)(2,1)} %param.9) | copy-start | bytes 400
  12.6 0.7 %copy-start.4 = (s32[2,2,2]{2,1,0:T(2,128)S(1)}, s32[2,2,2]{2,1,0:T(2,128)}, u32[]{:S(2)}) copy-start(s32[2,2,2]{2,1,0:T(2,128)} %brick_tf.1) | copy-start | bytes 100
  13.3 0.7 %copy-start.3 = (s32[2,2]{1,0:T(2,128)S(1)}, s32[2,2]{1,0:T(2,128)}, u32[]{:S(2)}) copy-start(s32[2,2]{1,0:T(2,128)} %view_order.3) | copy-start | bytes 52
  20.3 0.6 %copy-start.2 = (f32[4,8,32]{2,1,0:T(8,128)}, f32[4,8,32]{2,1,0:T(8,128)S(1)}, u32[]{:S(2)}) copy-start(f32[4,8,32]{2,1,0:T(8,128)S(1)} %get-tuple-element.31.refs_0_) | copy-start | bytes 12292
  20.9 3.5 %collective-permute-start.6 = (f32[4,8,32]{2,1,0:T(8,128)S(1)}, f32[4,8,32]{2,1,0:T(8,128)S(1)}, u32[]{:S(2)}, u32[]{:S(2)}) collective-permute-start(f32[4,8,32]{2,1,0:T(8,128)S(1)} %get-tuple-element.32), channel_id=1, source_target_pairs={{0,8},{8,0},{16,24},{24,16},{1,9},{9,1},{17,25},{25,17},{2,10},{10... | collective-permute-start | bytes 12296 | tf_op jit(solution)/shard_map/ppermute | solution.py:322
  22.7 2.6 %collective-permute-start.7 = (f32[4,8,32]{2,1,0:T(8,128)S(1)}, f32[4,8,32]{2,1,0:T(8,128)S(1)}, u32[]{:S(2)}, u32[]{:S(2)}) collective-permute-start(f32[4,8,32]{2,1,0:T(8,128)S(1)} %get-tuple-element.33), channel_id=1, source_target_pairs={{0,16},{8,24},{16,0},{24,8},{1,17},{9,25},{17,1},{25,9},{2,18},{10... | collective-permute-start | bytes 12296 | tf_op jit(solution)/shard_map/ppermute | solution.py:322
  23.9 3.2 %collective-permute-start.8 = (f32[4,8,32]{2,1,0:T(8,128)S(1)}, f32[4,8,32]{2,1,0:T(8,128)S(1)}, u32[]{:S(2)}, u32[]{:S(2)}) collective-permute-start(f32[4,8,32]{2,1,0:T(8,128)S(1)} %get-tuple-element.34), channel_id=1, source_target_pairs={{0,24},{8,16},{16,8},{24,0},{1,25},{9,17},{17,9},{25,1},{2,26},{10... | collective-permute-start | bytes 12296 | tf_op jit(solution)/shard_map/ppermute | solution.py:322
  24.3 2.7 %copy-start.5 = (f32[4,8,32]{2,1,0:T(8,128)}, f32[4,8,32]{2,1,0:T(8,128)S(1)}, u32[]{:S(2)}) copy-start(f32[4,8,32]{2,1,0:T(8,128)S(1)} %collective-permute-done.6.refs_1_) | copy-start | bytes 12292
  25.3 1.8 %copy-start.6 = (f32[4,8,32]{2,1,0:T(8,128)}, f32[4,8,32]{2,1,0:T(8,128)S(1)}, u32[]{:S(2)}) copy-start(f32[4,8,32]{2,1,0:T(8,128)S(1)} %collective-permute-done.7.refs_2_) | copy-start | bytes 12292
  27.1 0.6 %copy-start.7 = (f32[4,8,32]{2,1,0:T(8,128)}, f32[4,8,32]{2,1,0:T(8,128)S(1)}, u32[]{:S(2)}) copy-start(f32[4,8,32]{2,1,0:T(8,128)S(1)} %collective-permute-done.8.refs_3_) | copy-start | bytes 12292
where the time goes:
time: 29.5 us; the launch traced here: 29.1 us
  starting transfers between devices  12.9 us (44%)
  Pallas kernels  7.78 us (26%)
  local copies, waits for them, and re-layouts  4.63 us (16%)
  waiting for transfers between devices  3.74 us (13%)
    ppermute x2, starting transfers between devices, per_device(): lax.ppermute(piece, 'sx', swaps)  4.62 us
    unnamed x29, local copies, waits for them, and re-layouts  4.44 us
    pallas_call x1, Pallas kernels, per_device(): pl.pallas_call(functools.partial(cells_kernel, rim, bumps), grid=(bricks[...  4.25 us
    ppermute x3, starting transfers between devices, per_device(): lax.ppermute(parts[k], 'depth', [(i, i ^ k) for i in range(depth_count)])  3.46 us
    ppermute x2, starting transfers between devices, per_device(): lax.ppermute(strips[2 * r + n], 'sx', swaps)  3.26 us
    ppermute x3, waiting for transfers between devices, per_device(): lax.ppermute(parts[k], 'depth', [(i, i ^ k) for i in range(depth_count)])  2.74 us
    pallas_call x1, Pallas kernels, per_device(): pl.pallas_call(functools.partial(image_kernel, rim, depth_count, len(x_sw...  1.99 us
    ppermute x2, starting transfers between devices, per_device(): lax.ppermute(piece, 'sy', y_swaps[i // 2])  1.53 us
  transfers between devices with their start and end apart: 9, of which 3 were waited for; matrix products, arithmetic and copies ran while one was open for 1% of the time, Pallas kernels for 15%

commit v1 on v0

--- a/solution.py
+++ b/solution.py
@@ -66,7 +66,7 @@
 
 def cells_kernel(
     rim, bumps, taps, centre, width, colour, opacity, brick_tf, view_order, density,
-    coarse, g0, g1, g2, total, dd, ee, optical_s, e0, e1, e2
+    coarse, g0, g1, g2, total, dd, ee, optical_s, e0, e1, e2, padded
 ):
     by, bx = pl.program_id(0), pl.program_id(1)
     bricks = brick_tf.shape[2]
@@ -76,7 +76,9 @@
 
     @pl.when(jnp.logical_and(by == 0, bx == 0))
     def _():
-        dd_v, ee_v = blur_matrices(rim, taps[...])
+        padded[...] = jnp.zeros(padded.shape, f32)
+        padded[0:2, 0:taps.shape[1]] = taps[...].astype(f32)
+        dd_v, ee_v = blur_matrices(rim, padded[...])
         dd[...] = dd_v
         ee[...] = ee_v
 
@@ -87,11 +89,11 @@
         k = brick_tf[bx, by, bz]
         cen, neg, opa, col = [], [], [], []
         for j in range(bumps):
-            cen.append(centre[k, j])
-            wide = jnp.full((8, depth), width[k, j], f32)
+            cen.append(centre[j, k])
+            wide = jnp.full((8, depth), width[j, k], f32)
             neg.append((-LOG2E / (wide * wide))[None])
-            opa.append(opacity[k, j] * (-LOG2E))
-            col.append([colour[k, 3 * j + c] * 0.5 for c in range(3)])
+            opa.append(opacity[j, k] * (-LOG2E))
+            col.append([colour[c, j, k] * 0.5 for c in range(3)])
         for x in range(rows_x):
             d = density[x, :, zs].reshape(rows_y // 8, 8, depth)
             opt, em = None, [None] * 3
@@ -272,14 +274,7 @@
         lax.ppermute(piece, "sy", y_swaps[i // 2]) for i, piece in enumerate(sends[2:])
     ]
     x_halos = [lax.ppermute(piece, "sx", swaps) for piece, swaps in zip(sends[:2], x_swaps)]
-    corners = [
-        lax.ppermute(strips[2 * r + n], "sx", swaps)
-        for r in range(len(y_swaps))
-        for n, swaps in enumerate(x_swaps)
-    ]
-
     size = rim * rim
-    taps = jnp.pad(kernel_taps.astype(f32), ((0, 0), (0, 128 - kernel_taps.shape[1])))
     cell_block = pl.BlockSpec((rows_x // bricks[0], rows_y // bricks[1], rows_z), lambda y, x: (x, y, 0))
     whole = lambda shape: pl.BlockSpec(shape, lambda y, x: (0,) * len(shape))
     group_rows = (rows_x // bricks[0]) * (rows_y // bricks[1])
@@ -290,15 +285,22 @@
         + [struct(density.shape, f32)] * 3
         + [struct((rows_y, 128), f32)]
         + [struct((size, 3 * size), bf16)] * 2,
-        in_specs=[whole((2, 128))] + [SMEM] * 6 + [cell_block],
+        in_specs=[whole(kernel_taps.shape)] + [SMEM] * 6 + [cell_block],
         out_specs=[cell_block] * 4
         + [pl.BlockSpec((rows_y // bricks[1], 128), lambda y, x: (y, 0))]
         + [whole((size, 3 * size))] * 2,
-        scratch_shapes=[pltpu.VMEM((group_rows, rows_z), f32)] * 4,
+        scratch_shapes=[pltpu.VMEM((group_rows, rows_z), f32)] * 4 + [pltpu.VMEM((8, 128), f32)],
         compiler_params=params,
         cost_estimate=pl.CostEstimate(flops=density.size * 60, bytes_accessed=density.size * 20, transcendentals=density.size * 6),
         name="cells",
-    )(taps, tf_centre, tf_width, tf_color.reshape(tf_color.shape[0], -1), tf_opacity, brick_tf, view_order, density)
+    )(kernel_taps, tf_centre.T, tf_width.T, tf_color.T, tf_opacity.T, brick_tf, view_order, density)
+
+    strips, dd = lax.optimization_barrier((strips, dd))
+    corners = [
+        lax.ppermute(strips[2 * r + n], "sx", swaps)
+        for r in range(len(y_swaps))
+        for n, swaps in enumerate(x_swaps)
+    ]
 
     block = rows_x // depth_count
     n_copies = 1 + len(x_swaps) + 2 * len(y_swaps) + len(corners)
@@ -327,6 +329,7 @@
         out_shape=struct((4, 1, 1, block, rows_y), f32),
         in_specs=[SMEM] + [VMEM] * depth_count,
         out_specs=VMEM,
+        compiler_params=pltpu.CompilerParams(vmem_limit_bytes=2 * 1024 * 1024),
         name="picture",
     )(view_order, *pieces)
 

time: 29.5 us -> 29.5 us (level)
  waiting for transfers between devices: 3.74 us -> 6.75 us
  local copies, waits for them, and re-layouts: 4.63 us -> 2.54 us
  starting transfers between devices: 12.9 us -> 12.4 us
  Pallas kernels: 7.78 us -> 7.41 us
    ppermute x2, waiting for transfers between devices: 0.01 us -> 4.06 us  [per_device(): lax.ppermute(strips[2 * r + n], 'sx', swaps)]
    unnamed x29 -> x18, local copies, waits for them, and re-layouts: 4.44 us -> 2.54 us
    ppermute x2, starting transfers between devices: 3.26 us -> 1.99 us  [per_device(): lax.ppermute(strips[2 * r + n], 'sx', swaps)]
    ppermute x2, waiting for transfers between devices: 0.99 us -> 0.01 us  [per_device(): lax.ppermute(piece, 'sy', y_swaps[i // 2])]
    ppermute x3, starting transfers between devices: 3.46 us -> 4.42 us  [per_device(): lax.ppermute(parts[k], 'depth', [(i, i ^ k) for i in range(depth_count)])]
  transfers between devices with their start and end apart: 9 -> 9, of which waited for: 3 -> 4; matrix products, arithmetic and copies ran while one was open for 1% -> 0% of each run, Pallas kernels for 15% -> 14%
where the time goes in v1:
time: 29.5 us; the launch traced here: 29.3 us
  starting transfers between devices  12.4 us (42%)
  Pallas kernels  7.41 us (25%)
  waiting for transfers between devices  6.75 us (23%)
  local copies, waits for them, and re-layouts  2.54 us (9%)
    ppermute x2, starting transfers between devices, per_device(): lax.ppermute(piece, 'sx', swaps)  4.49 us
    ppermute x3, starting transfers between devices, per_device(): lax.ppermute(parts[k], 'depth', [(i, i ^ k) for i in range(depth_count)])  4.42 us
    pallas_call x1, Pallas kernels, per_device(): pl.pallas_call(functools.partial(cells_kernel, rim, bumps), grid=(bricks[...  4.23 us
    ppermute x2, waiting for transfers between devices, per_device(): lax.ppermute(strips[2 * r + n], 'sx', swaps)  4.06 us
    ppermute x3, waiting for transfers between devices, per_device(): lax.ppermute(parts[k], 'depth', [(i, i ^ k) for i in range(depth_count)])  2.68 us
    unnamed x18, local copies, waits for them, and re-layouts  2.54 us
    ppermute x2, starting transfers between devices, per_device(): lax.ppermute(strips[2 * r + n], 'sx', swaps)  1.99 us
    pallas_call x1, Pallas kernels, per_device(): pl.pallas_call(functools.partial(image_kernel, rim, depth_count, len(x_sw...  1.92 us
  transfers between devices with their start and end apart: 9, of which 4 were waited for; matrix products, arithmetic and copies ran while one was open for 0% of the time, Pallas kernels for 14%

profile of v1, /device:TPU:13, one launch (start us, length us, event | category | flops | bytes accessed | tf_op | source)
XLA Modules:
  0.0 29.3 jit_solution(2224026948203747376)
XLA Ops:
  0.0 1.2 %copy-done = f32[32,32,256]{2,1,0:T(8,128)S(1)} copy-done((f32[32,32,256]{2,1,0:T(8,128)S(1)}, f32[32,32,256]{2,1,0:T(8,128)}, u32[]{:S(2)}) %copy-start) | copy-done | bytes 1048600
  1.2 0.1 strips.1
  1.3 0.0 copy-start.5
  1.3 0.0 copy-start.6
  1.3 0.3 collective-permute-start
  1.6 1.2 %collective-permute-start.1 = (bf16[16,16,256]{2,1,0:T(8,128)(2,1)S(1)}, bf16[16,16,256]{2,1,0:T(8,128)(2,1)S(1)}, u32[]{:S(2)}, u32[]{:S(2)}) collective-permute-start(bf16[16,16,256]{2,1,0:T(8,128)(2,1)S(1)} %get-tuple-element.29), channel_id=1, source_target_pairs={{0,1},{1,0},{2,3},{3,2},{4,5},{5,4},{6,7},{7,6},{8,9},{9,8},{10,11... | collective-permute-start | bytes 393224 | tf_op jit(solution)/shard_map/ppermute | solution.py:274
  2.9 0.2 collective-permute-start.2
  3.0 4.3 %collective-permute-start.3 = (bf16[16,32,256]{2,1,0:T(8,128)(2,1)S(1)}, bf16[16,32,256]{2,1,0:T(8,128)(2,1)S(1)}, u32[]{:S(2)}, u32[]{:S(2)}) collective-permute-start(bf16[16,32,256]{2,1,0:T(8,128)(2,1)S(1)} %get-tuple-element.34), channel_id=1, source_target_pairs={{2,4},{4,2},{3,5},{5,3},{10,12},{12,10},{11,13},{13,11},{18,20},{2... | collective-permute-start | bytes 786440 | tf_op jit(solution)/shard_map/ppermute | solution.py:276
  7.4 0.0 copy-start.2
  7.5 0.6 %copy-done.4 = f32[8,4]{0,1:T(4,128)S(1)} copy-done((f32[8,4]{0,1:T(4,128)S(1)}, f32[8,4]{0,1:T(4,128)}, u32[]{:S(2)}) %copy-start.4) | copy-done | bytes 152
  8.1 0.0 copy-done.2
  8.1 0.7 %copy-done.8 = bf16[2,33]{1,0:T(2,128)(2,1)S(1)} copy-done((bf16[2,33]{1,0:T(2,128)(2,1)S(1)}, bf16[2,33]{1,0:T(2,128)(2,1)}, u32[]{:S(2)}) %copy-start.8) | copy-done | bytes 156
  8.7 4.2 %cells.1 = (bf16[32,32,256]{2,1,0:T(8,128)(2,1)S(1)}, f32[32,32,256]{2,1,0:T(8,128)S(1)}, f32[32,32,256]{2,1,0:T(8,128)S(1)}, f32[32,32,256]{2,1,0:T(8,128)S(1)}...) custom-call(bf16[2,33]{1,0:T(2,128)(2,1)S(1)} %copy-done.8, ...), custom_call_target="tpu_custom_call" | custom-call | flops 15728640 | bytes 5242880 | tf_op jit(solution)/shard_map/cells/pallas_call | solution.py:281
  13.0 0.1 collective-permute-start.4
  13.1 1.9 %collective-permute-start.5 = (bf16[16,16,256]{2,1,0:T(8,128)(2,1)S(1)}, bf16[16,16,256]{2,1,0:T(8,128)(2,1)S(1)}, u32[]{:S(2)}, u32[]{:S(2)}) collective-permute-start(bf16[16,16,256]{2,1,0:T(8,128)(2,1)S(1)} %collective-permute-done.1.refs_10_), channel_id=1, source_target_pairs={{2,4},{4,2},{3,5},{5,3},{10,12},{12,10},{11,13},{13,11},{18,20},{2... | collective-permute-start | bytes 393224 | tf_op jit(solution)/shard_map/ppermute | solution.py:300
  15.0 1.9 %collective-permute-done.4.refs_11_ = bf16[16,16,256]{2,1,0:T(8,128)(2,1)S(1)} collective-permute-done((bf16[16,16,256]{2,1,0:T(8,128)(2,1)S(1)}, bf16[16,16,256]{2,1,0:T(8,128)(2,1)S(1)}, u32[]{:S(2)}, u32[]{:S(2)}) %collective-permute-start.4) | collective-permute-done | bytes 131104 | tf_op jit(solution)/shard_map/ppermute | solution.py:300
  16.9 2.2 %collective-permute-done.5.refs_12_ = bf16[16,16,256]{2,1,0:T(8,128)(2,1)S(1)} collective-permute-done((bf16[16,16,256]{2,1,0:T(8,128)(2,1)S(1)}, bf16[16,16,256]{2,1,0:T(8,128)(2,1)S(1)}, u32[]{:S(2)}, u32[]{:S(2)}) %collective-permute-start.5) | collective-permute-done | bytes 131104 | tf_op jit(solution)/shard_map/ppermute | solution.py:300
  19.1 1.9 %image.1 = (f32[4,8,32]{2,1,0:T(8,128)S(1)}, f32[4,8,32]{2,1,0:T(8,128)S(1)}, f32[4,8,32]{2,1,0:T(8,128)S(1)}, f32[4,8,32]{2,1,0:T(8,128)S(1)}) custom-call(bf16[32,32,256]{2,1,0:T(8,128)(2,1)S(1)} %get-tuple-element.23.refs_0_, f32[32,32,256]{2,1,0:T(8,128)S(1)} %get-tuple-element.24.refs_1_, f32[32,32,256]{2,1,0:T(8,128)S(1)} %get-tuple-element.25.refs_2_, ...), custom_call_target="tpu_custom_call" | custom-call | tf_op jit(solution)/shard_map/image/pallas_call | solution.py:307
  21.0 2.7 %collective-permute-start.6 = (f32[4,8,32]{2,1,0:T(8,128)S(1)}, f32[4,8,32]{2,1,0:T(8,128)S(1)}, u32[]{:S(2)}, u32[]{:S(2)}) collective-permute-start(f32[4,8,32]{2,1,0:T(8,128)S(1)} %get-tuple-element.38), channel_id=1, source_target_pairs={{0,8},{8,0},{16,24},{24,16},{1,9},{9,1},{17,25},{25,17},{2,10},{10... | collective-permute-start | bytes 12296 | tf_op jit(solution)/shard_map/ppermute | solution.py:324
  23.7 1.2 %collective-permute-start.7 = (f32[4,8,32]{2,1,0:T(8,128)S(1)}, f32[4,8,32]{2,1,0:T(8,128)S(1)}, u32[]{:S(2)}, u32[]{:S(2)}) collective-permute-start(f32[4,8,32]{2,1,0:T(8,128)S(1)} %get-tuple-element.39), channel_id=1, source_target_pairs={{0,16},{8,24},{16,0},{24,8},{1,17},{9,25},{17,1},{25,9},{2,18},{10... | collective-permute-start | bytes 12296 | tf_op jit(solution)/shard_map/ppermute | solution.py:324
  24.9 0.5 %collective-permute-start.8 = (f32[4,8,32]{2,1,0:T(8,128)S(1)}, f32[4,8,32]{2,1,0:T(8,128)S(1)}, u32[]{:S(2)}, u32[]{:S(2)}) collective-permute-start(f32[4,8,32]{2,1,0:T(8,128)S(1)} %get-tuple-element.40), channel_id=1, source_target_pairs={{0,24},{8,16},{16,8},{24,0},{1,25},{9,17},{17,9},{25,1},{2,26},{10... | collective-permute-start | bytes 12296 | tf_op jit(solution)/shard_map/ppermute | solution.py:324
  25.4 0.9 %collective-permute-done.7.refs_2_ = f32[4,8,32]{2,1,0:T(8,128)S(1)} collective-permute-done((f32[4,8,32]{2,1,0:T(8,128)S(1)}, f32[4,8,32]{2,1,0:T(8,128)S(1)}, u32[]{:S(2)}, u32[]{:S(2)}) %collective-permute-start.7) | collective-permute-done | bytes 4128 | tf_op jit(solution)/shard_map/ppermute | solution.py:324
  26.3 1.8 %collective-permute-done.8.refs_3_ = f32[4,8,32]{2,1,0:T(8,128)S(1)} collective-permute-done((f32[4,8,32]{2,1,0:T(8,128)S(1)}, f32[4,8,32]{2,1,0:T(8,128)S(1)}, u32[]{:S(2)}, u32[]{:S(2)}) %collective-permute-start.8) | collective-permute-done | bytes 4128 | tf_op jit(solution)/shard_map/ppermute | solution.py:324
  28.1 1.2 %picture.1 = f32[4,1,1,8,32]{4,3,2,1,0:T(8,128)} custom-call(s32[2,2]{1,0:T(2,128)S(1)} %copy-done.2, f32[4,8,32]{2,1,0:T(8,128)S(1)} %get-tuple-element.37.refs_0_, f32[4,8,32]{2,1,0:T(8,128)S(1)} %collective-permute-done.6.refs_1_, f32[4,8,32]{2,1,0:T(8,128)S(1)} %collective-permute-done.7.refs_2_, f32[4,8,32]{2,1,0:T(8,128)S(1)} %collective-permute-done.8.refs_3_), custom_call_target="tpu_custom_call" | custom-call | tf_op jit(solution)/shard_map/picture/pallas_call | solution.py:327
  (16 shorter events, 0.0 us)
Async XLA Ops:
  0.0 1.2 %copy-start = (f32[32,32,256]{2,1,0:T(8,128)S(1)}, f32[32,32,256]{2,1,0:T(8,128)}, u32[]{:S(2)}) copy-start(f32[32,32,256]{2,1,0:T(8,128)} %density.3) | copy-start | bytes 3145732
  1.2 6.2 %copy-start.1 = (f32[32,32,256]{2,1,0:T(8,128)S(1)}, f32[32,32,256]{2,1,0:T(8,128)}, u32[]{:S(2)}) copy-start(f32[32,32,256]{2,1,0:T(8,128)} %density.3) | copy-start | bytes 3145732
  1.3 6.1 %copy-start.5 = (f32[8,4]{0,1:T(4,128)S(1)}, f32[8,4]{0,1:T(4,128)}, u32[]{:S(2)}) copy-start(f32[8,4]{0,1:T(4,128)} %param.11) | copy-start | bytes 388
  1.3 6.1 %copy-start.6 = (f32[8,4]{0,1:T(4,128)S(1)}, f32[8,4]{0,1:T(4,128)}, u32[]{:S(2)}) copy-start(f32[8,4]{0,1:T(4,128)} %param.13) | copy-start | bytes 388
  1.3 6.1 %copy-start.7 = (s32[2,2,2]{2,1,0:T(2,128)S(1)}, s32[2,2,2]{2,1,0:T(2,128)}, u32[]{:S(2)}) copy-start(s32[2,2,2]{2,1,0:T(2,128)} %brick_tf.1) | copy-start | bytes 100
  1.3 11.6 %collective-permute-start = (bf16[16,16,256]{2,1,0:T(8,128)(2,1)S(1)}, bf16[16,16,256]{2,1,0:T(8,128)(2,1)S(1)}, u32[]{:S(2)}, u32[]{:S(2)}) collective-permute-start(bf16[16,16,256]{2,1,0:T(8,128)(2,1)S(1)} %get-tuple-element.28), channel_id=1, source_target_pairs={{0,1},{1,0},{2,3},{3,2},{4,5},{5,4},{6,7},{7,6},{8,9},{9,8},{10,11... | collective-permute-start | bytes 393224 | tf_op jit(solution)/shard_map/ppermute | solution.py:274
  1.6 5.8 %copy-start.3 = (f32[8,4,3]{0,1,2:T(4,128)S(1)}, f32[8,4,3]{0,1,2:T(4,128)}, u32[]{:S(2)}) copy-start(f32[8,4,3]{0,1,2:T(4,128)} %param.12) | copy-start | bytes 1156
  1.6 11.3 %collective-permute-start.1 = (bf16[16,16,256]{2,1,0:T(8,128)(2,1)S(1)}, bf16[16,16,256]{2,1,0:T(8,128)(2,1)S(1)}, u32[]{:S(2)}, u32[]{:S(2)}) collective-permute-start(bf16[16,16,256]{2,1,0:T(8,128)(2,1)S(1)} %get-tuple-element.29), channel_id=1, source_target_pairs={{0,1},{1,0},{2,3},{3,2},{4,5},{5,4},{6,7},{7,6},{8,9},{9,8},{10,11... | collective-permute-start | bytes 393224 | tf_op jit(solution)/shard_map/ppermute | solution.py:274
  2.9 12.1 %collective-permute-start.2 = (bf16[16,32,256]{2,1,0:T(8,128)(2,1)S(1)}, bf16[16,32,256]{2,1,0:T(8,128)(2,1)S(1)}, u32[]{:S(2)}, u32[]{:S(2)}) collective-permute-start(bf16[16,32,256]{2,1,0:T(8,128)(2,1)S(1)} %get-tuple-element.33), channel_id=1, source_target_pairs={{0,2},{4,6},{2,0},{6,4},{1,3},{5,7},{3,1},{7,5},{8,10},{12,14},{10... | collective-permute-start | bytes 786440 | tf_op jit(solution)/shard_map/ppermute | solution.py:276
  3.0 12.0 %collective-permute-start.3 = (bf16[16,32,256]{2,1,0:T(8,128)(2,1)S(1)}, bf16[16,32,256]{2,1,0:T(8,128)(2,1)S(1)}, u32[]{:S(2)}, u32[]{:S(2)}) collective-permute-start(bf16[16,32,256]{2,1,0:T(8,128)(2,1)S(1)} %get-tuple-element.34), channel_id=1, source_target_pairs={{2,4},{4,2},{3,5},{5,3},{10,12},{12,10},{11,13},{13,11},{18,20},{2... | collective-permute-start | bytes 786440 | tf_op jit(solution)/shard_map/ppermute | solution.py:276
  7.4 0.7 %copy-start.4 = (f32[8,4]{0,1:T(4,128)S(1)}, f32[8,4]{0,1:T(4,128)}, u32[]{:S(2)}) copy-start(f32[8,4]{0,1:T(4,128)} %param.10) | copy-start | bytes 388
  7.4 0.7 %copy-start.2 = (s32[2,2]{1,0:T(2,128)S(1)}, s32[2,2]{1,0:T(2,128)}, u32[]{:S(2)}) copy-start(s32[2,2]{1,0:T(2,128)} %view_order.3) | copy-start | bytes 52
  8.1 0.7 %copy-start.8 = (bf16[2,33]{1,0:T(2,128)(2,1)S(1)}, bf16[2,33]{1,0:T(2,128)(2,1)}, u32[]{:S(2)}) copy-start(bf16[2,33]{1,0:T(2,128)(2,1)} %taps.1) | copy-start | bytes 400
  13.0 3.9 %collective-permute-start.4 = (bf16[16,16,256]{2,1,0:T(8,128)(2,1)S(1)}, bf16[16,16,256]{2,1,0:T(8,128)(2,1)S(1)}, u32[]{:S(2)}, u32[]{:S(2)}) collective-permute-start(bf16[16,16,256]{2,1,0:T(8,128)(2,1)S(1)} %collective-permute-done.refs_9_), channel_id=1, source_target_pairs={{0,2},{4,6},{2,0},{6,4},{1,3},{5,7},{3,1},{7,5},{8,10},{12,14},{10... | collective-permute-start | bytes 393224 | tf_op jit(solution)/shard_map/ppermute | solution.py:300
  13.1 6.0 %collective-permute-start.5 = (bf16[16,16,256]{2,1,0:T(8,128)(2,1)S(1)}, bf16[16,16,256]{2,1,0:T(8,128)(2,1)S(1)}, u32[]{:S(2)}, u32[]{:S(2)}) collective-permute-start(bf16[16,16,256]{2,1,0:T(8,128)(2,1)S(1)} %collective-permute-done.1.refs_10_), channel_id=1, source_target_pairs={{2,4},{4,2},{3,5},{5,3},{10,12},{12,10},{11,13},{13,11},{18,20},{2... | collective-permute-start | bytes 393224 | tf_op jit(solution)/shard_map/ppermute | solution.py:300
  21.0 4.4 %collective-permute-start.6 = (f32[4,8,32]{2,1,0:T(8,128)S(1)}, f32[4,8,32]{2,1,0:T(8,128)S(1)}, u32[]{:S(2)}, u32[]{:S(2)}) collective-permute-start(f32[4,8,32]{2,1,0:T(8,128)S(1)} %get-tuple-element.38), channel_id=1, source_target_pairs={{0,8},{8,0},{16,24},{24,16},{1,9},{9,1},{17,25},{25,17},{2,10},{10... | collective-permute-start | bytes 12296 | tf_op jit(solution)/shard_map/ppermute | solution.py:324
  23.7 2.6 %collective-permute-start.7 = (f32[4,8,32]{2,1,0:T(8,128)S(1)}, f32[4,8,32]{2,1,0:T(8,128)S(1)}, u32[]{:S(2)}, u32[]{:S(2)}) collective-permute-start(f32[4,8,32]{2,1,0:T(8,128)S(1)} %get-tuple-element.39), channel_id=1, source_target_pairs={{0,16},{8,24},{16,0},{24,8},{1,17},{9,25},{17,1},{25,9},{2,18},{10... | collective-permute-start | bytes 12296 | tf_op jit(solution)/shard_map/ppermute | solution.py:324
  24.9 3.2 %collective-permute-start.8 = (f32[4,8,32]{2,1,0:T(8,128)S(1)}, f32[4,8,32]{2,1,0:T(8,128)S(1)}, u32[]{:S(2)}, u32[]{:S(2)}) collective-permute-start(f32[4,8,32]{2,1,0:T(8,128)S(1)} %get-tuple-element.40), channel_id=1, source_target_pairs={{0,24},{8,16},{16,8},{24,0},{1,25},{9,17},{17,9},{25,1},{2,26},{10... | collective-permute-start | bytes 12296 | tf_op jit(solution)/shard_map/ppermute | solution.py:324
